TPU v7x, 32 devices: a whole 2x2x4 slice. The times are simulated.
32 devices in a mesh: groups: 2 (over x), expert: 4 (over z), tensor: 4 (over y, core).
Axes of the slice: x: 2, y: 2, z: 4, core: 2. Of those that a mesh axis runs over, the one named last changes fastest.
Arguments:
- context: bfloat16 [512, 3072], P(('groups', 'expert'), 'tensor'), parts along dimension 0, may hold values from -6 to 6
- out_proj: bfloat16 [3072, 3072], P('tensor'), may hold values from -0.109375 to 0.109375
- resid: bfloat16 [512, 3072], P(('groups', 'expert')), parts along dimension 0, may hold values from -6 to 6
- norm_gain: bfloat16 [3072], replicated, may hold values from 0.099609375 to 1.8984375
- routes: int32 [512, 2], P(('groups', 'expert')), parts along dimension 0, may hold values from 0 to 3, all different within a row; in each aligned block of 16 rows (0 to 15, 16 to 31, ...) at most 8 rows name the same one
- gates: float32 [512, 2], P(('groups', 'expert', 'tensor')), parts along dimension 0, may hold values from 0.1 to 1
- w_gate: bfloat16 [4, 3072, 8192], P('expert', None, 'tensor'), may hold values from -0.109375 to 0.109375
- w_up: bfloat16 [4, 3072, 8192], P('expert', None, 'tensor'), may hold values from -0.109375 to 0.109375
- w_down: bfloat16 [4, 8192, 3072], P('expert', 'tensor'), may hold values from -0.0625 to 0.0625
Outputs:
- mixed: bfloat16 [512, 3072], P(('groups', 'expert', 'tensor')), parts along dimension 0
There are 2 independent parts, one for each index of `groups`. A program takes and returns all parts, laid end to end along the dimension named above; an argument that names none is the same for every part. Nothing has to cross between parts.
Inputs may be any that keep to these rules, and one draw needn't show every extreme that they name: `routes`: the two experts of a row differ; in each aligned block of 16 rows (the rows of one device) no expert is named by more than 8 rows.
All inputs are finite; a program needn't handle non-finite values.
Results may differ from a plain program's by a relative error of at most 0.0041.
Values may be sent and summed in bfloat16 or wider, within the bound.
A program may use at most 128 MiB of HBM per device.

v0:
```python
import jax
import jax.numpy as jnp
from jax import lax
from jax.sharding import PartitionSpec as P


def normalize(state, norm_gain):
    scale = lax.rsqrt(jnp.mean(state * state, axis=-1, keepdims=True) + 1e-05)
    return (state * scale * norm_gain.astype(jnp.float32)).astype(jnp.bfloat16)


def body(context, out_proj, resid, norm_gain, routes, gates, w_gate, w_up, w_down):
    tok_rows = gates.shape[0]
    width = resid.shape[1]
    capacity = tok_rows // 2
    tparts = lax.axis_size("tensor")
    tplace = lax.axis_index("tensor")
    experts = lax.axis_size("expert")
    flat_routes = routes.reshape(tparts, tok_rows * 2)
    onehot = (
        flat_routes[:, :, None] == jnp.arange(experts, dtype=jnp.int32)[None, None, :]
    ).astype(jnp.int32)
    before = jnp.cumsum(onehot, axis=1) - onehot
    slots = jnp.sum(before * onehot, axis=-1).reshape(tparts * tok_rows, 2)
    own_routes = lax.dynamic_slice_in_dim(routes, tplace * tok_rows, tok_rows, 0)
    own_slots = lax.dynamic_slice_in_dim(slots, tplace * tok_rows, tok_rows, 0)
    own_dest = own_routes * capacity + own_slots
    ffdev = w_gate.shape[2]
    rows = context
    attn = lax.psum_scatter(
        jnp.dot(rows, out_proj, preferred_element_type=jnp.float32),
        "tensor",
        scatter_dimension=0,
        tiled=True,
    )
    own_resid = lax.dynamic_slice_in_dim(resid, tplace * tok_rows, tok_rows, 0)
    state = own_resid.astype(jnp.float32) + attn
    normed = normalize(state, norm_gain)
    send = jnp.zeros((experts * capacity, width), jnp.bfloat16)
    send = send.at[own_dest[:, 0]].set(normed).at[own_dest[:, 1]].set(normed)
    received = lax.all_to_all(
        send.reshape(experts, 1, capacity, width), "expert", split_axis=0, concat_axis=0, tiled=True
    )
    piece = lax.all_gather(received, "tensor", axis=1, tiled=True)
    lead = piece.shape[:-1]
    rows = piece.reshape(-1, width)
    gate = jnp.dot(rows, w_gate[0], preferred_element_type=jnp.float32)
    upper = jnp.dot(rows, w_up[0], preferred_element_type=jnp.float32)
    hidden = (jax.nn.silu(gate) * upper).astype(jnp.bfloat16)
    hidden = hidden.reshape(lead + (ffdev,))
    partial_value = jnp.dot(
        hidden.reshape(-1, ffdev), w_down[0], preferred_element_type=jnp.float32
    )
    partial_value = partial_value.reshape(experts, tparts, capacity, width)
    summed = lax.psum_scatter(partial_value, "tensor", scatter_dimension=1, tiled=True).astype(
        jnp.bfloat16
    )
    returned = lax.all_to_all(summed, "expert", split_axis=0, concat_axis=0, tiled=True)
    flat_out = returned.reshape(experts * capacity, width)
    first = flat_out[own_dest[:, 0]].astype(jnp.float32)
    second = flat_out[own_dest[:, 1]].astype(jnp.float32)
    mixed = state + gates[:, 0:1] * first + gates[:, 1:2] * second
    return mixed.astype(jnp.bfloat16)


def solution(mesh):
    in_specs = (
        P(("groups", "expert"), "tensor"),
        P("tensor", None),
        P(("groups", "expert"), None),
        P(),
        P(("groups", "expert"), None),
        P(("groups", "expert", "tensor"), None),
        P("expert", None, "tensor"),
        P("expert", None, "tensor"),
        P("expert", "tensor", None),
    )
    out_specs = P(("groups", "expert", "tensor"), None)
    return jax.shard_map(body, mesh=mesh, in_specs=in_specs, out_specs=out_specs, check_vma=False)
```

profile of v0, /device:TPU:0, one launch (start us, length us, event | category | flops | bytes accessed | tf_op | source)
XLA Modules:
  0.0 129.7 jit_solution(13205708889696683759)
XLA Ops:
  6.5 0.0 copy-start
  6.5 0.0 reduce-scatter.3.cloned.1.call-start
  6.5 0.9 copy-done
  7.4 4.1 %fusion.17 = f32[64,3072]{1,0:T(8,128)} fusion(bf16[64,768]{1,0:T(8,128)(2,1)S(1)} %copy-done, bf16[768,3072]{1,0:T(8,128)(2,1)} %param.10), kind=kOutput, calls=%fused_computation.32 | convolution fusion | flops 301989888 | bytes 5603328 | tf_op jit(solution)/shard_map/dot_general | solution.py:31
  11.6 0.0 reduce-scatter.3.cloned.1.call-update
  11.6 0.7 convert_element_type.29
  12.3 0.8 copy.14
  13.1 0.1 eq.15
  13.2 0.1 fusion.14
  13.3 0.1 reduce_window_sum.11
  13.3 0.2 select_reduce_fusion
  13.5 0.1 reshape.24
  13.7 0.2 fusion.16
  13.8 23.8 %reduce-scatter.3.cloned.1.call-done = f32[16,3072]{1,0:T(8,128)} async-done(((f32[64,3072]{1,0:T(8,128)}), f32[16,3072]{1,0:T(8,128)}) %reduce-scatter.3.cloned.1.call-update) | async-done | bytes 196624 | tf_op jit(solution)/shard_map/reduce_scatter | solution.py:30
  37.7 1.1 multiply_reduce_fusion
  38.8 1.1 multiply_convert_fusion
  39.9 1.4 %scatter_custom_fusion = bf16[32,3072]{1,0:T(8,128)(2,1)} fusion(s32[16]{0:T(128)S(1)} %get-tuple-element.6, bf16[16,3072]{1,0:T(8,128)(2,1)S(1)} %multiply_convert_fusion, bf16[]{:T(256)} %constant.7.clone.1), kind=kCustom, calls=%fused_computation.17 | custom fusion | bytes 196610 | tf_op jit(solution)/shard_map/scatter | solution.py:40
  41.3 2.3 %scatter_fusion = bf16[32,3072]{1,0:T(8,128)(2,1)} fusion(bf16[32,3072]{1,0:T(8,128)(2,1)} %scatter_custom_fusion, s32[16]{0:T(128)S(1)} %get-tuple-element.5, bf16[16,3072]{1,0:T(8,128)(2,1)S(1)} %multiply_convert_fusion), kind=kCustom, calls=%fused_computation.3 | custom fusion | bytes 294976 | tf_op jit(solution)/shard_map/scatter | solution.py:40
  43.6 4.6 %all-to-all-start = ((bf16[4,1,8,3072]{3,2,1,0:T(8,128)(2,1)}), bf16[4,1,8,3072]{3,2,1,0:T(8,128)(2,1)S(1)}, u32[]{:S(2)}, u32[]{:S(2)}) async-start(bf16[4,1,8,3072]{3,2,1,0:T(8,128)(2,1)} %bitcast.1), calls=%async_computation.1 | async-start | bytes 393216 | tf_op jit(solution)/shard_map/all_to_all | solution.py:41
  48.2 1.2 dynamic-slice
  49.5 6.3 %all-to-all-done = bf16[4,1,8,3072]{3,2,1,0:T(8,128)(2,1)S(1)} async-done(((bf16[4,1,8,3072]{3,2,1,0:T(8,128)(2,1)}), bf16[4,1,8,3072]{3,2,1,0:T(8,128)(2,1)S(1)}, u32[]{:S(2)}, u32[]{:S(2)}) %all-to-all-start) | async-done | bytes 196640 | tf_op jit(solution)/shard_map/all_to_all | solution.py:41
  55.7 0.0 copy-start.3
  55.7 7.8 %all_gather.3 = bf16[4,4,8,3072]{3,2,1,0:T(8,128)(2,1)S(1)} all-gather(bf16[4,1,8,3072]{3,2,1,0:T(8,128)(2,1)S(1)} %all-to-all-done), channel_id=1, replica_groups=mesh['groups'=2,'expert'=4,'tensor'=4] {'tensor'}, dimensions={1}, use_global_device_ids=true | all-gather | bytes 983040 | tf_op jit(solution)/shard_map/all_gather | solution.py:44
  63.5 0.0 slice-start
  63.5 0.0 slice-start.1
  63.5 6.6 %fusion.4 = f32[128,2048]{1,0:T(8,128)S(1)} fusion(bf16[128,3072]{1,0:T(8,128)(2,1)S(1)} %bitcast.37, bf16[1,3072,2048]{2,1,0:T(8,128)(2,1)} %param.15), kind=kOutput, calls=%fused_computation.8 | convolution fusion | flops 1610612736 | bytes 14417920 | tf_op jit(solution)/shard_map/dot_general | solution.py:47
  70.1 0.0 copy-done.3
  70.1 0.0 slice-start.2
  70.1 2.1 %fusion.9 = bf16[128,2048]{1,0:T(8,128)(2,1)S(1)} fusion(bf16[128,3072]{1,0:T(8,128)(2,1)S(1)} %bitcast.38, bf16[1,3072,2048]{2,1,0:T(8,128)(2,1)S(1)} %copy-done.3, f32[128,2048]{1,0:T(8,128)S(1)} %fusion.4), kind=kOutput, calls=%fused_computation.11 | convolution fusion | flops 1612185600 | bytes 14942208 | tf_op jit(solution)/shard_map/dot_general | solution.py:48
  72.3 0.0 copy-start.2
  72.3 0.0 copy-start.1
  72.3 0.0 slice-done
  72.3 0.0 slice-done.1
  72.3 0.1 slice-done.2
  72.4 2.0 %fusion = f32[4,4,8,3072]{3,2,1,0:T(8,128)S(1)} fusion(bf16[4,4,8,2048]{3,2,1,0:T(8,128)(2,1)S(1)} %bitcast.39, bf16[1,2048,3072]{2,1,0:T(8,128)(2,1)S(1)} %bitcast.34), kind=kOutput, calls=%fused_computation.4 | convolution fusion | flops 1610612736 | bytes 14680064 | tf_op jit(solution)/shard_map/dot_general | solution.py:51
  74.4 32.8 %all-reduce.2 = bf16[4,4,8,3072]{3,2,1,0:T(8,128)(2,1)S(1)} all-reduce(f32[4,4,8,3072]{3,2,1,0:T(8,128)S(1)} %fusion), channel_id=3, replica_groups=mesh['groups'=2,'expert'=4,'tensor'=4] {'tensor'}, use_global_device_ids=true, to_apply=%region_6.7.clone | all-reduce | flops 393216 | bytes 2359296
  107.2 1.3 %dynamic-slice_convert_fusion = bf16[4,1,8,3072]{3,2,1,0:T(8,128)(2,1)} fusion(bf16[4,4,8,3072]{3,2,1,0:T(8,128)(2,1)S(1)} %all-reduce.2, u32[]{:T(128)} %bitcast.15), kind=kLoop, calls=%fused_computation.12 | loop fusion | bytes 393220 | tf_op jit(solution)/shard_map/convert_element_type | solution.py:55
  108.5 3.4 %all-to-all-start.1 = ((bf16[4,1,8,3072]{3,2,1,0:T(8,128)(2,1)}), bf16[4,1,8,3072]{3,2,1,0:T(8,128)(2,1)S(1)}, u32[]{:S(2)}, u32[]{:S(2)}) async-start(bf16[4,1,8,3072]{3,2,1,0:T(8,128)(2,1)} %dynamic-slice_convert_fusion), calls=%async_computation.2 | async-start | bytes 393216 | tf_op jit(solution)/shard_map/all_to_all | solution.py:58
  111.9 0.0 copy-done.2
  111.9 8.0 %all-to-all-done.1 = bf16[4,1,8,3072]{3,2,1,0:T(8,128)(2,1)S(1)} async-done(((bf16[4,1,8,3072]{3,2,1,0:T(8,128)(2,1)}), bf16[4,1,8,3072]{3,2,1,0:T(8,128)(2,1)S(1)}, u32[]{:S(2)}, u32[]{:S(2)}) %all-to-all-start.1) | async-done | bytes 196640 | tf_op jit(solution)/shard_map/all_to_all | solution.py:58
  119.9 0.6 gather_fusion
  120.5 0.6 gather_fusion.1
  121.2 0.0 copy-done.1
  121.2 1.7 %add_convert_fusion = bf16[16,3072]{1,0:T(8,128)(2,1)} fusion(bf16[16,3072]{1,0:T(8,128)(2,1)S(1)} %gather_fusion.1, bf16[16,3072]{1,0:T(8,128)(2,1)S(1)} %gather_fusion, f32[16]{0:T(128)S(1)} %get-tuple-element.8, f32[16]{0:T(128)S(1)} %get-tuple-element.7, f32[16,3072]{1,0:T(8,128)S(1)} %copy-done.1, bf16[64,3072]{1,0:T(8,128)(2,1)} %param.11, s32[]{:T(128)S(6)} %select_n.15), kind=kLoop, calls=%fused_computation.13 | loop fusion | flops 442368 | bytes 589956 | tf_op jit(solution)/shard_map/convert_element_type | solution.py:63
  (5 shorter events, 0.0 us)
Async XLA Ops:
  6.5 0.9 copy-start
  6.5 31.2 %reduce-scatter.3.cloned.1.call-start = ((), (), s32[]{:S(2)}) async-start(), calls=%async_computation.3 | async-start | bytes 983040 | tf_op jit(solution)/shard_map/reduce_scatter | solution.py:30
  43.6 12.1 %all-to-all-start = ((bf16[4,1,8,3072]{3,2,1,0:T(8,128)(2,1)}), bf16[4,1,8,3072]{3,2,1,0:T(8,128)(2,1)S(1)}, u32[]{:S(2)}, u32[]{:S(2)}) async-start(bf16[4,1,8,3072]{3,2,1,0:T(8,128)(2,1)} %bitcast.1), calls=%async_computation.1 | async-start | bytes 393216 | tf_op jit(solution)/shard_map/all_to_all | solution.py:41
  55.7 14.4 %copy-start.3 = (bf16[1,3072,2048]{2,1,0:T(8,128)(2,1)S(1)}, bf16[1,3072,2048]{2,1,0:T(8,128)(2,1)}, u32[]{:S(2)}) copy-start(bf16[1,3072,2048]{2,1,0:T(8,128)(2,1)} %param.16) | copy-start | bytes 37748740
  63.5 8.8 %slice-start = ((s8[12582912]{0:T(1024)(128)(4,1)}), s8[4194304]{0:T(1024)(128)(4,1)S(1)}, s32[]{:S(2)}) async-start(s8[12582912]{0:T(1024)(128)(4,1)} %bitcast.33), calls=%async_computation.4 | async-start | bytes 8388608
  63.5 8.8 %slice-start.1 = ((s8[12582912]{0:T(1024)(128)(4,1)}), s8[4194304]{0:T(1024)(128)(4,1)S(1)}, s32[]{:S(2)}) async-start(s8[12582912]{0:T(1024)(128)(4,1)} %bitcast.33), calls=%async_computation.5 | async-start | bytes 8388608
  70.1 2.3 %slice-start.2 = ((s8[12582912]{0:T(1024)(128)(4,1)}), s8[4194304]{0:T(1024)(128)(4,1)S(1)}, s32[]{:S(2)}) async-start(s8[12582912]{0:T(1024)(128)(4,1)} %bitcast.33), calls=%async_computation.6 | async-start | bytes 8388608
  72.3 39.6 %copy-start.2 = (f32[16,2]{0,1:T(2,128)S(1)}, f32[16,2]{0,1:T(2,128)}, u32[]{:S(2)}) copy-start(f32[16,2]{0,1:T(2,128)} %param.14) | copy-start | bytes 388
  72.3 48.9 %copy-start.1 = (f32[16,3072]{1,0:T(8,128)S(1)}, f32[16,3072]{1,0:T(8,128)}, u32[]{:S(2)}) copy-start(f32[16,3072]{1,0:T(8,128)} %reduce-scatter.3.cloned.1.call-done) | copy-start | bytes 589828
  108.5 11.4 %all-to-all-start.1 = ((bf16[4,1,8,3072]{3,2,1,0:T(8,128)(2,1)}), bf16[4,1,8,3072]{3,2,1,0:T(8,128)(2,1)S(1)}, u32[]{:S(2)}, u32[]{:S(2)}) async-start(bf16[4,1,8,3072]{3,2,1,0:T(8,128)(2,1)} %dynamic-slice_convert_fusion), calls=%async_computation.2 | async-start | bytes 393216 | tf_op jit(solution)/shard_map/all_to_all | solution.py:58
Sparse Core Ops, SparseCore 0:
  11.7 25.9 reduce-scatter.2
where the time goes:
time: 130 us
  blocking collectives  40.6 us (31%)
  waiting for transfers between devices  38.1 us (29%)
  matrix products  14.8 us (11%)
  between operations  13.6 us (10%)
  local copies, waits for them, and re-layouts  9.45 us (7%)
  starting transfers between devices  7.98 us (6%)
  other arithmetic  5.14 us (4%)
    unnamed x1, blocking collectives  32.8 us
    reduce_scatter x1, waiting for transfers between devices, body(): lax.psum_scatter(jnp.dot(rows, out_proj, preferred_element_type=jnp.float...  23.8 us
    all_to_all x1, waiting for transfers between devices, body(): lax.all_to_all(summed, 'expert', split_axis=0, concat_axis=0, tiled=True)  7.99 us
    all_gather x1, blocking collectives, body(): piece = lax.all_gather(received, 'tensor', axis=1, tiled=True)  7.76 us
    dot_general x1, matrix products, body(): gate = jnp.dot(rows, w_gate[0], preferred_element_type=jnp.float32)  6.58 us
    all_to_all x1, waiting for transfers between devices, body(): lax.all_to_all(send.reshape(experts, 1, capacity, width), 'expert', split...  6.28 us
    all_to_all x1, starting transfers between devices, body(): lax.all_to_all(send.reshape(experts, 1, capacity, width), 'expert', split...  4.61 us
    dot_general x1, matrix products, body(): jnp.dot(rows, out_proj, preferred_element_type=jnp.float32)  4.15 us
  transfers between devices with their start and end apart: 3, of which 3 were waited for; matrix products, arithmetic and copies ran while one was open for 3% of the time, Pallas kernels for 0%

commit v1 on v0

v1 whole, which is shorter than its diff:
```python
import functools

import jax
import jax.numpy as jnp
from jax import lax
from jax.experimental import pallas as pl
from jax.experimental.pallas import tpu as pltpu
from jax.sharding import PartitionSpec as P

MESH = pl.DeviceIdType.MESH
F32 = jnp.float32
BF16 = jnp.bfloat16
CHUNKS = 4


def kernel(
    n_exp, n_ten,
    ctx_hbm, proj_hbm, resid_hbm, gain_ref, routes_ref, gates_ref, wg_hbm, wu_hbm, wd_hbm,
    out_ref,
    ctx, proj, resid, wg, wu, wd,
    part, pa_out, pa_in, pb_out, pb_in,
    state, pack, rows, lhs, acc_g, acc_u, hid,
    part2, qa_out, qa_in, qb_out, qb_in, ret_out, ret_in,
    load_sem, proj_sem, gate_sem, up_sem, down_sem,
    pas, par, pbs, pbr, zs, zr, cs, cr, ys, yr, fs, fr, qas, qar, qbs, qbr, rs, rr,
):
    e = lax.axis_index("expert")
    t = lax.axis_index("tensor")
    core = lax.rem(t, 2)
    y = t // 2
    ny = n_ten // 2
    mate = y * 2 + 1 - core
    tok = state.shape[0]
    width = state.shape[1]
    cap = tok // 2
    slots = n_exp * cap
    dc = width // CHUNKS
    half = dc // 2
    total = n_ten * slots
    ff = wg.shape[1]

    def remote(src, dst, send, recv, where):
        copy = pltpu.make_async_remote_copy(
            src_ref=src, dst_ref=dst, send_sem=send, recv_sem=recv,
            device_id=where, device_id_type=MESH,
        )
        return copy

    def cols(c):
        return pl.ds(c * dc, dc)

    first_loads = [
        pltpu.make_async_copy(ctx_hbm, ctx, load_sem.at[0]),
        pltpu.make_async_copy(
            resid_hbm.at[pl.ds(pl.multiple_of(t * tok, tok), tok)], resid, load_sem.at[1]
        ),
    ]
    proj_loads = [
        pltpu.make_async_copy(proj_hbm.at[:, cols(c)], proj.at[:, cols(c)], proj_sem.at[c])
        for c in range(CHUNKS)
    ]
    gate_loads = [
        pltpu.make_async_copy(wg_hbm.at[0, cols(c)], wg.at[cols(c)], gate_sem.at[c])
        for c in range(CHUNKS)
    ]
    up_loads = [
        pltpu.make_async_copy(wu_hbm.at[0, cols(c)], wu.at[cols(c)], up_sem.at[c])
        for c in range(CHUNKS)
    ]
    down_loads = [
        pltpu.make_async_copy(wd_hbm.at[0, :, cols(c)], wd.at[:, cols(c)], down_sem.at[c])
        for c in range(CHUNKS)
    ]
    for load in first_loads + proj_loads:
        load.start()
    for c in range(CHUNKS):
        gate_loads[c].start()
        up_loads[c].start()
    for load in down_loads:
        load.start()

    others_y = [lax.rem(y + k, ny) for k in range(1, ny)]
    others_e = [lax.rem(e + k, n_exp) for k in range(1, n_exp)]

    barrier = pltpu.get_barrier_semaphore()
    pl.semaphore_signal(barrier, inc=1, device_id={"tensor": mate}, device_id_type=MESH)
    for oy in others_y:
        pl.semaphore_signal(
            barrier, inc=1, device_id={"tensor": oy * 2 + core}, device_id_type=MESH
        )
    for oe in others_e:
        pl.semaphore_signal(barrier, inc=1, device_id={"expert": oe}, device_id_type=MESH)

    own = routes_ref[pl.ds(pl.multiple_of(t * tok, tok), tok), :]
    lane = lax.broadcasted_iota(jnp.int32, (tok, 128), 1)
    lane_exp = lane // cap
    lane_slot = (lane - lane_exp * cap).astype(F32)
    m0 = jnp.where(own[:, 0:1] == lane_exp, 1.0, 0.0).astype(F32)
    m1 = jnp.where(own[:, 1:2] == lane_exp, 1.0, 0.0).astype(F32)
    ri = lax.broadcasted_iota(jnp.int32, (tok, tok), 0)
    ci = lax.broadcasted_iota(jnp.int32, (tok, tok), 1)
    lower = jnp.where(ci < ri, 1.0, 0.0).astype(BF16)
    before = jnp.dot(lower, (m0 + m1).astype(BF16), preferred_element_type=F32)
    hit = jnp.where(before == lane_slot, 1.0, 0.0)
    s0 = (m0 * hit)[:, :slots].astype(BF16)
    s1 = (m1 * hit)[:, :slots].astype(BF16)
    spread = ((m0 + m1) * hit)[:, :slots].astype(BF16)

    for load in first_loads:
        load.wait()
    pl.semaphore_wait(barrier, 1 + (ny - 1) + (n_exp - 1))

    sends = []

    def reduce_a(buf, c, out, into, send, recv):
        for oy in range(ny):
            out[c, oy] = buf[c, oy * 2 + 1 - core].astype(BF16)
        copy = remote(out.at[c], into.at[c], send.at[c], recv.at[c], {"tensor": mate})
        copy.start()
        sends.append(copy)
        return copy

    def reduce_b(buf, c, into, out, into2, send, recv):
        copies = []
        for k in range(1, ny):
            oy = others_y[k - 1]
            out[c, k - 1] = (buf[c, oy * 2 + core] + into[c, oy].astype(F32)).astype(BF16)
            copy = remote(
                out.at[c, k - 1], into2.at[c, k - 1], send.at[c, k - 1], recv.at[c, k - 1],
                {"tensor": oy * 2 + core},
            )
            copy.start()
            sends.append(copy)
            copies.append(copy)
        return copies

    def reduce_c(buf, c, into, into2):
        value = buf[c, t] + into[c, y].astype(F32)
        for k in range(1, ny):
            value = value + into2[c, k - 1].astype(F32)
        return value

    def fold(value):
        value = value.reshape(n_exp, cap, value.shape[-1])
        side = value.shape[-1] // 2
        return jnp.concatenate([value[:, :, :side], value[:, :, side:]], axis=1)

    def spans(c):
        wide = half + (128 if c == CHUNKS - 1 else 0)
        return pl.ds(c * half, wide)

    square = [jnp.zeros((tok, 1), F32)]
    pa, pb, pz, pc, py, pf = {}, {}, {}, {}, {}, {}

    def stage_a(c):
        proj_loads[c].wait()
        nt = half
        ctx_rows = ctx.shape[0]
        for n in range(dc // nt):
            sl = pl.ds(c * dc + n * nt, nt)
            value = jnp.dot(ctx[...], proj[:, sl], preferred_element_type=F32)
            part[c, :, :, n * nt:(n + 1) * nt] = value.reshape(n_ten, ctx_rows // n_ten, nt)
        pa[c] = reduce_a(part, c, pa_out, pa_in, pas, par)

    def stage_b(c):
        pa[c].wait_recv()
        pb[c] = reduce_b(part, c, pa_in, pb_out, pb_in, pbs, pbr)

    def stage_c(c):
        for copy in pb[c]:
            copy.wait_recv()
        sl = cols(c)
        value = resid[:, sl].astype(F32) + reduce_c(part, c, pa_in, pb_in)
        state[:, sl] = value
        square[0] = square[0] + jnp.sum(value * value, axis=1, keepdims=True)
        x = (value * gain_ref[:, sl].astype(F32)).astype(BF16)
        dims = (((0,), (0,)), ((), ()))
        packed = lax.dot_general(spread, x, dims, preferred_element_type=F32)
        pack[:, :, c * half:(c + 1) * half] = fold(packed).astype(BF16)
        if c == CHUNKS - 1:
            scale = lax.rsqrt(square[0] / width + 1e-05)
            scale = jnp.broadcast_to(scale, (tok, 128))
            high = scale.astype(BF16)
            low = (scale - high.astype(F32)).astype(BF16)
            both = jnp.concatenate([high, low], axis=1)
            packed = lax.dot_general(spread, both, dims, preferred_element_type=F32)
            pack[:, :, width // 2:] = fold(packed).astype(BF16)
        sp = spans(c)
        pz[c] = []
        for k in range(1, n_exp):
            oe = others_e[k - 1]
            copy = remote(
                pack.at[oe, :, sp], rows.at[t, e, :, sp], zs.at[c, k - 1], zr.at[c, k - 1],
                {"expert": oe},
            )
            copy.start()
            sends.append(copy)
            pz[c].append(copy)
        rows[t, e, :, sp] = pack[e, :, sp]

    def stage_d(c):
        for copy in pz[c]:
            copy.wait_recv()
        sp = spans(c)
        pieces = rows.at[t, :, :, sp]
        py[c] = []
        for k in range(1, ny):
            copy = remote(
                pieces, pieces, ys.at[c, k - 1], yr.at[c, k - 1],
                {"tensor": others_y[k - 1] * 2 + core},
            )
            copy.start()
            sends.append(copy)
            py[c].append(copy)
        pc[c] = remote(pieces, pieces, cs.at[c], cr.at[c], {"tensor": mate})
        pc[c].start()
        sends.append(pc[c])

    def stage_e(c):
        sp = spans(c)
        pf[c] = []
        for k in range(1, ny):
            py[c][k - 1].wait_recv()
            src = lax.rem(y - k + ny, ny) * 2 + core
            pieces = rows.at[src, :, :, sp]
            copy = remote(
                pieces, pieces, fs.at[c, k - 1], fr.at[c, k - 1], {"tensor": mate}
            )
            copy.start()
            sends.append(copy)
            pf[c].append(copy)

    mb = min(total, 128)
    nt = min(ff, 512)

    def stage_f(c):
        pc[c].wait_recv()
        for copy in pf[c]:
            copy.wait_recv()
        last = c == CHUNKS - 1
        sp = pl.ds(c * half, half)

        def unfold(i, _):
            value = rows[i, :, :, sp].astype(F32)
            at = pl.ds(pl.multiple_of(i * slots, slots), slots)
            lhs[at, c * dc:c * dc + half] = value[:, :cap].reshape(slots, half).astype(BF16)
            lhs[at, c * dc + half:(c + 1) * dc] = (
                value[:, cap:].reshape(slots, half).astype(BF16)
            )
            return 0

        lax.fori_loop(0, n_ten, unfold, 0, unroll=True)
        gate_loads[c].wait()
        up_loads[c].wait()

        def block(m, _):
            at = pl.ds(pl.multiple_of(m * mb, mb), mb)
            if last:
                per = mb // slots
                tail = rows[pl.ds(m * per, per), :, :, width // 2:].astype(F32)
                scale = (tail[:, :, :cap] + tail[:, :, cap:]).reshape(mb, 128)[:, 0:1]

            def tile(n, _):
                cs_ = pl.ds(pl.multiple_of(n * nt, nt), nt)
                left = lhs[at, cols(c)]
                g = jnp.dot(left, wg[cols(c), cs_], preferred_element_type=F32)
                u = jnp.dot(left, wu[cols(c), cs_], preferred_element_type=F32)
                if c > 0:
                    g = g + acc_g[at, cs_]
                    u = u + acc_u[at, cs_]
                if last:
                    g = g * scale
                    u = u * scale
                    hid[at, cs_] = (g / (1.0 + jnp.exp(-g)) * u).astype(BF16)
                else:
                    acc_g[at, cs_] = g
                    acc_u[at, cs_] = u
                return 0

            lax.fori_loop(0, ff // nt, tile, 0)
            return 0

        lax.fori_loop(0, total // mb, block, 0)

    order = [stage_a, stage_b, stage_c, stage_d, stage_e, stage_f]
    for s in range(CHUNKS + len(order) - 1):
        for depth, stage in enumerate(order):
            if 0 <= s - depth < CHUNKS:
                stage(s - depth)

    qa, qb, pr = {}, {}, {}

    def down_a(c):
        down_loads[c].wait()
        per = mb // slots
        wt = half

        def block(m, _):
            at = pl.ds(pl.multiple_of(m * mb, mb), mb)
            for n in range(dc // wt):
                sl = pl.ds(c * dc + n * wt, wt)
                value = jnp.dot(hid[at, :], wd[:, sl], preferred_element_type=F32)
                part2[c, pl.ds(m * per, per), :, n * wt:(n + 1) * wt] = value.reshape(
                    per, slots, wt
                )
            return 0

        lax.fori_loop(0, total // mb, block, 0)
        qa[c] = reduce_a(part2, c, qa_out, qa_in, qas, qar)

    def down_b(c):
        qa[c].wait_recv()
        qb[c] = reduce_b(part2, c, qa_in, qb_out, qb_in, qbs, qbr)

    def down_c(c):
        for copy in qb[c]:
            copy.wait_recv()
        ret_out[c] = fold(reduce_c(part2, c, qa_in, qb_in)).astype(BF16)
        pr[c] = []
        for k in range(1, n_exp):
            oe = others_e[k - 1]
            copy = remote(
                ret_out.at[c, oe], ret_in.at[c, e], rs.at[c, k - 1], rr.at[c, k - 1],
                {"expert": oe},
            )
            copy.start()
            sends.append(copy)
            pr[c].append(copy)
        ret_in[c, e] = ret_out[c, e]

    def down_d(c):
        for copy in pr[c]:
            copy.wait_recv()
        value = ret_in[c].astype(F32)
        for side in range(2):
            piece = value[:, side * cap:(side + 1) * cap].reshape(slots, half).astype(BF16)
            sl = pl.ds(c * dc + side * half, half)
            first = jnp.dot(s0, piece, preferred_element_type=F32)
            second = jnp.dot(s1, piece, preferred_element_type=F32)
            mixed = state[:, sl] + gates_ref[:, 0:1] * first + gates_ref[:, 1:2] * second
            out_ref[:, sl] = mixed.astype(BF16)

    order = [down_a, down_b, down_c, down_d]
    for s in range(CHUNKS + len(order) - 1):
        for depth, stage in enumerate(order):
            if 0 <= s - depth < CHUNKS:
                stage(s - depth)

    for copy in sends:
        copy.wait_send()


def body(context, out_proj, resid, norm_gain, routes, gates, w_gate, w_up, w_down):
    n_exp = lax.axis_size("expert")
    n_ten = lax.axis_size("tensor")
    ny = n_ten // 2
    tok = gates.shape[0]
    width = resid.shape[1]
    cap = tok // 2
    slots = n_exp * cap
    total = n_ten * slots
    ff = w_gate.shape[2]
    dc = width // CHUNKS
    half = dc // 2
    lanes = width // 2 + 128
    dma = pltpu.SemaphoreType.DMA
    hbm = pl.BlockSpec(memory_space=pl.ANY)
    vmem = pl.BlockSpec(memory_space=pltpu.VMEM)
    many = max(ny - 1, 1)
    return pl.pallas_call(
        functools.partial(kernel, n_exp, n_ten),
        out_shape=jax.ShapeDtypeStruct((tok, width), BF16),
        in_specs=[hbm, hbm, hbm, vmem, vmem, vmem, hbm, hbm, hbm],
        out_specs=vmem,
        scratch_shapes=[
            pltpu.VMEM(context.shape, BF16),
            pltpu.VMEM(out_proj.shape, BF16),
            pltpu.VMEM((tok, width), BF16),
            pltpu.VMEM((width, ff), BF16),
            pltpu.VMEM((width, ff), BF16),
            pltpu.VMEM((ff, width), BF16),
            pltpu.VMEM((CHUNKS, n_ten, tok, dc), F32),
            pltpu.VMEM((CHUNKS, ny, tok, dc), BF16),
            pltpu.VMEM((CHUNKS, ny, tok, dc), BF16),
            pltpu.VMEM((CHUNKS, many, tok, dc), BF16),
            pltpu.VMEM((CHUNKS, many, tok, dc), BF16),
            pltpu.VMEM((tok, width), F32),
            pltpu.VMEM((n_exp, 2 * cap, lanes), BF16),
            pltpu.VMEM((n_ten, n_exp, 2 * cap, lanes), BF16),
            pltpu.VMEM((total, width), BF16),
            pltpu.VMEM((total, ff), F32),
            pltpu.VMEM((total, ff), F32),
            pltpu.VMEM((total, ff), BF16),
            pltpu.VMEM((CHUNKS, n_ten, slots, dc), F32),
            pltpu.VMEM((CHUNKS, ny, slots, dc), BF16),
            pltpu.VMEM((CHUNKS, ny, slots, dc), BF16),
            pltpu.VMEM((CHUNKS, many, slots, dc), BF16),
            pltpu.VMEM((CHUNKS, many, slots, dc), BF16),
            pltpu.VMEM((CHUNKS, n_exp, 2 * cap, half), BF16),
            pltpu.VMEM((CHUNKS, n_exp, 2 * cap, half), BF16),
            dma((2,)),
            dma((CHUNKS,)),
            dma((CHUNKS,)),
            dma((CHUNKS,)),
            dma((CHUNKS,)),
            dma((CHUNKS,)),
            dma((CHUNKS,)),
            dma((CHUNKS, many)),
            dma((CHUNKS, many)),
            dma((CHUNKS, n_exp - 1)),
            dma((CHUNKS, n_exp - 1)),
            dma((CHUNKS,)),
            dma((CHUNKS,)),
            dma((CHUNKS, many)),
            dma((CHUNKS, many)),
            dma((CHUNKS, many)),
            dma((CHUNKS, many)),
            dma((CHUNKS,)),
            dma((CHUNKS,)),
            dma((CHUNKS, many)),
            dma((CHUNKS, many)),
            dma((CHUNKS, n_exp - 1)),
            dma((CHUNKS, n_exp - 1)),
        ],
        compiler_params=pltpu.CompilerParams(
            collective_id=0, has_side_effects=True, vmem_limit_bytes=62 * 1024 * 1024
        ),
    )(
        context, out_proj, resid, norm_gain.reshape(1, width), routes, gates,
        w_gate, w_up, w_down,
    )


def solution(mesh):
    in_specs = (
        P(("groups", "expert"), "tensor"),
        P("tensor", None),
        P(("groups", "expert"), None),
        P(),
        P(("groups", "expert"), None),
        P(("groups", "expert", "tensor"), None),
        P("expert", None, "tensor"),
        P("expert", None, "tensor"),
        P("expert", "tensor", None),
    )
    out_specs = P(("groups", "expert", "tensor"), None)
    return jax.shard_map(body, mesh=mesh, in_specs=in_specs, out_specs=out_specs, check_vma=False)
```

time: 130 us -> 59.7 us (0.46)
  Pallas kernels: 0 us -> 53.8 us
  blocking collectives: 40.6 us -> 0 us
  waiting for transfers between devices: 38.1 us -> 0 us
  matrix products: 14.8 us -> 0 us
  between operations: 13.6 us -> 0.01 us
  starting transfers between devices: 7.98 us -> 0 us
  other arithmetic: 5.14 us -> 0 us
  local copies, waits for them, and re-layouts: 9.45 us -> 5.57 us
    pallas_call x0 -> x1, Pallas kernels: none -> 53.8 us  [body(): pl.pallas_call(functools.partial(kernel, n_exp, n_ten), out_shape=jax.Sha...]
    unnamed x1 -> x0, blocking collectives: 32.8 us -> none
    reduce_scatter x1 -> x0, waiting for transfers between devices: 23.8 us -> none  [body(): lax.psum_scatter(jnp.dot(rows, out_proj, preferred_element_type=jnp.float...]
    dot_general x4 -> x0, matrix products: 14.8 us -> none  [the longest x1 6.58 us: body(): gate = jnp.dot(rows, w_gate[0], preferred_element_type=jnp.float32)]
    all_to_all x2 -> x0, waiting for transfers between devices: 14.3 us -> none  [the longest x1 7.99 us: body(): lax.all_to_all(summed, 'expert', split_axis=0, concat_axis=0, tiled=True)]
    all_to_all x2 -> x0, starting transfers between devices: 7.98 us -> none  [the longest x1 4.61 us: body(): lax.all_to_all(send.reshape(experts, 1, capacity, width), 'expert', split...]
    all_gather x1 -> x0, blocking collectives: 7.76 us -> none  [body(): piece = lax.all_gather(received, 'tensor', axis=1, tiled=True)]
    scatter x2 -> x0, local copies, waits for them, and re-layouts: 3.7 us -> none  [body(): send = send.at[own_dest[:, 0]].set(normed).at[own_dest[:, 1]].set(normed)]
  transfers between devices with their start and end apart: 3 -> 0, of which waited for: 3 -> 0; matrix products, arithmetic and copies ran while one was open for 3% -> 0% of each run, Pallas kernels for 0% -> 0%
where the time goes in v1:
time: 59.7 us; the launch traced here: 59.4 us
  Pallas kernels  53.8 us (90%)
  local copies, waits for them, and re-layouts  5.57 us (9%)
    pallas_call x1, Pallas kernels, body(): pl.pallas_call(functools.partial(kernel, n_exp, n_ten), out_shape=jax.Sha...  53.8 us
    unnamed x3, local copies, waits for them, and re-layouts  4.28 us
    reshape x1, local copies, waits for them, and re-layouts, body(): norm_gain.reshape(1, width)  1.3 us

profile of v1, /device:TPU:0, one launch (start us, length us, event | category | flops | bytes accessed | tf_op | source)
XLA Modules:
  0.0 59.4 jit_solution(11139984026996238508)
XLA Ops:
  0.0 1.4 %copy.11.gates_ref = f32[16,2]{1,0:T(8,128)} copy(f32[16,2]{0,1:T(2,128)} %param.14) | data formatting | bytes 256 | tf_op args[5]
  1.4 1.3 %reshape.3.gain_ref = bf16[1,3072]{1,0:T(2,128)(2,1)} reshape(bf16[3072]{0:T(1024)(128)(2,1)} %param.12) | data formatting | bytes 12288 | tf_op jit(solution)/shard_map/reshape | solution.py:429
  2.7 1.4 %copy.10.routes_ref = s32[64,2]{1,0:T(8,128)} copy(s32[64,2]{0,1:T(2,128)} %param.13) | data formatting | bytes 1024 | tf_op args[4]
  4.0 53.8 %shard_map.91 = bf16[16,3072]{1,0:T(8,128)(2,1)} custom-call(bf16[64,768]{1,0:T(8,128)(2,1)} %ctx_hbm.1, bf16[768,3072]{1,0:T(8,128)(2,1)} %proj_hbm.1, bf16[64,3072]{1,0:T(8,128)(2,1)} %resid_hbm.1, bf16[1,3072]{1,0:T(2,128)(2,1)} %reshape.3.gain_ref, s32[64,2]{1,0:T(8,128)} %copy.10.routes_ref, f32[16,2]{1,0:T(8,128)} %copy.11.gates_ref, ...), custom_call_target="tpu_custom_call" | custom-call | tf_op jit(solution)/shard_map/pallas_call | solution.py:370
  57.9 1.5 %copy.13 = bf16[16,3072]{1,0:T(8,128)(2,1)} copy(bf16[16,3072]{1,0:T(8,128)(2,1)} %shard_map.91) | data formatting | bytes 196608

commit v2 on v1

--- a/solution.py
+++ b/solution.py
@@ -10,7 +10,8 @@
 MESH = pl.DeviceIdType.MESH
 F32 = jnp.float32
 BF16 = jnp.bfloat16
-CHUNKS = 4
+CHUNKS = 2
+BACK = 2
 
 
 def kernel(
@@ -36,6 +37,8 @@
     slots = n_exp * cap
     dc = width // CHUNKS
     half = dc // 2
+    dc2 = width // BACK
+    half2 = dc2 // 2
     total = n_ten * slots
     ff = wg.shape[1]
 
@@ -67,17 +70,7 @@
         pltpu.make_async_copy(wu_hbm.at[0, cols(c)], wu.at[cols(c)], up_sem.at[c])
         for c in range(CHUNKS)
     ]
-    down_loads = [
-        pltpu.make_async_copy(wd_hbm.at[0, :, cols(c)], wd.at[:, cols(c)], down_sem.at[c])
-        for c in range(CHUNKS)
-    ]
-    for load in first_loads + proj_loads:
-        load.start()
-    for c in range(CHUNKS):
-        gate_loads[c].start()
-        up_loads[c].start()
-    for load in down_loads:
-        load.start()
+    down_load = pltpu.make_async_copy(wd_hbm.at[0], wd, down_sem.at[0])
 
     others_y = [lax.rem(y + k, ny) for k in range(1, ny)]
     others_e = [lax.rem(e + k, n_exp) for k in range(1, n_exp)]
@@ -91,12 +84,24 @@
     for oe in others_e:
         pl.semaphore_signal(barrier, inc=1, device_id={"expert": oe}, device_id_type=MESH)
 
-    own = routes_ref[pl.ds(pl.multiple_of(t * tok, tok), tok), :]
+    for load in first_loads + proj_loads:
+        load.start()
+
+    def column(row, start):
+        spot = lax.broadcasted_iota(jnp.int32, (tok, row.shape[1]), 1)
+        line = lax.broadcasted_iota(jnp.int32, (tok, row.shape[1]), 0)
+        return jnp.sum(jnp.where(spot == line + start, row, 0.0), axis=1, keepdims=True)
+
+    chosen = routes_ref[...].astype(F32)
+    weights = gates_ref[...]
+    gate0, gate1 = column(weights[0:1], 0), column(weights[1:2], 0)
+    route0 = column(chosen[0:1], t * tok).astype(jnp.int32)
+    route1 = column(chosen[1:2], t * tok).astype(jnp.int32)
     lane = lax.broadcasted_iota(jnp.int32, (tok, 128), 1)
     lane_exp = lane // cap
     lane_slot = (lane - lane_exp * cap).astype(F32)
-    m0 = jnp.where(own[:, 0:1] == lane_exp, 1.0, 0.0).astype(F32)
-    m1 = jnp.where(own[:, 1:2] == lane_exp, 1.0, 0.0).astype(F32)
+    m0 = jnp.where(route0 == lane_exp, 1.0, 0.0).astype(F32)
+    m1 = jnp.where(route1 == lane_exp, 1.0, 0.0).astype(F32)
     ri = lax.broadcasted_iota(jnp.int32, (tok, tok), 0)
     ci = lax.broadcasted_iota(jnp.int32, (tok, tok), 1)
     lower = jnp.where(ci < ri, 1.0, 0.0).astype(BF16)
@@ -108,8 +113,6 @@
 
     for load in first_loads:
         load.wait()
-    pl.semaphore_wait(barrier, 1 + (ny - 1) + (n_exp - 1))
-
     sends = []
 
     def reduce_a(buf, c, out, into, send, recv):
@@ -160,7 +163,13 @@
             sl = pl.ds(c * dc + n * nt, nt)
             value = jnp.dot(ctx[...], proj[:, sl], preferred_element_type=F32)
             part[c, :, :, n * nt:(n + 1) * nt] = value.reshape(n_ten, ctx_rows // n_ten, nt)
+        if c == 0:
+            pl.semaphore_wait(barrier, 1 + (ny - 1) + (n_exp - 1))
         pa[c] = reduce_a(part, c, pa_out, pa_in, pas, par)
+        if c == CHUNKS - 1:
+            for load in [x for pair in zip(gate_loads, up_loads) for x in pair]:
+                load.start()
+            down_load.start()
 
     def stage_b(c):
         pa[c].wait_recv()
@@ -173,7 +182,7 @@
         value = resid[:, sl].astype(F32) + reduce_c(part, c, pa_in, pb_in)
         state[:, sl] = value
         square[0] = square[0] + jnp.sum(value * value, axis=1, keepdims=True)
-        x = (value * gain_ref[:, sl].astype(F32)).astype(BF16)
+        x = (value * gain_ref[sl].astype(F32).reshape(1, dc)).astype(BF16)
         dims = (((0,), (0,)), ((), ()))
         packed = lax.dot_general(spread, x, dims, preferred_element_type=F32)
         pack[:, :, c * half:(c + 1) * half] = fold(packed).astype(BF16)
@@ -198,44 +207,50 @@
             pz[c].append(copy)
         rows[t, e, :, sp] = pack[e, :, sp]
 
+    hops = sorted(range(n_exp), key=lambda k: min(k, n_exp - k))
+
     def stage_d(c):
-        for copy in pz[c]:
-            copy.wait_recv()
         sp = spans(c)
-        pieces = rows.at[t, :, :, sp]
-        py[c] = []
-        for k in range(1, ny):
-            copy = remote(
-                pieces, pieces, ys.at[c, k - 1], yr.at[c, k - 1],
-                {"tensor": others_y[k - 1] * 2 + core},
-            )
+        py[c], pc[c] = {}, []
+        for k in hops:
+            if k > 0:
+                pz[c][k - 1].wait_recv()
+            src = lax.rem(e - k + n_exp, n_exp)
+            piece = rows.at[t, src, :, sp]
+            for q in range(1, ny):
+                copy = remote(
+                    piece, piece, ys.at[c, k, q - 1], yr.at[c, k, q - 1],
+                    {"tensor": others_y[q - 1] * 2 + core},
+                )
+                copy.start()
+                sends.append(copy)
+                py[c][k, q] = copy
+            copy = remote(piece, piece, cs.at[c, k], cr.at[c, k], {"tensor": mate})
             copy.start()
             sends.append(copy)
-            py[c].append(copy)
-        pc[c] = remote(pieces, pieces, cs.at[c], cr.at[c], {"tensor": mate})
-        pc[c].start()
-        sends.append(pc[c])
+            pc[c].append(copy)
 
     def stage_e(c):
         sp = spans(c)
         pf[c] = []
-        for k in range(1, ny):
-            py[c][k - 1].wait_recv()
-            src = lax.rem(y - k + ny, ny) * 2 + core
-            pieces = rows.at[src, :, :, sp]
-            copy = remote(
-                pieces, pieces, fs.at[c, k - 1], fr.at[c, k - 1], {"tensor": mate}
-            )
-            copy.start()
-            sends.append(copy)
-            pf[c].append(copy)
+        for k in hops:
+            src = lax.rem(e - k + n_exp, n_exp)
+            for q in range(1, ny):
+                py[c][k, q].wait_recv()
+                far = lax.rem(y - q + ny, ny) * 2 + core
+                piece = rows.at[far, src, :, sp]
+                copy = remote(
+                    piece, piece, fs.at[c, k, q - 1], fr.at[c, k, q - 1], {"tensor": mate}
+                )
+                copy.start()
+                sends.append(copy)
+                pf[c].append(copy)
 
     mb = min(total, 128)
     nt = min(ff, 512)
 
     def stage_f(c):
-        pc[c].wait_recv()
-        for copy in pf[c]:
+        for copy in pc[c] + pf[c]:
             copy.wait_recv()
         last = c == CHUNKS - 1
         sp = pl.ds(c * half, half)
@@ -291,14 +306,15 @@
     qa, qb, pr = {}, {}, {}
 
     def down_a(c):
-        down_loads[c].wait()
+        if c == 0:
+            down_load.wait()
         per = mb // slots
-        wt = half
+        wt = half2
 
         def block(m, _):
             at = pl.ds(pl.multiple_of(m * mb, mb), mb)
-            for n in range(dc // wt):
-                sl = pl.ds(c * dc + n * wt, wt)
+            for n in range(dc2 // wt):
+                sl = pl.ds(c * dc2 + n * wt, wt)
                 value = jnp.dot(hid[at, :], wd[:, sl], preferred_element_type=F32)
                 part2[c, pl.ds(m * per, per), :, n * wt:(n + 1) * wt] = value.reshape(
                     per, slots, wt
@@ -333,17 +349,17 @@
             copy.wait_recv()
         value = ret_in[c].astype(F32)
         for side in range(2):
-            piece = value[:, side * cap:(side + 1) * cap].reshape(slots, half).astype(BF16)
-            sl = pl.ds(c * dc + side * half, half)
+            piece = value[:, side * cap:(side + 1) * cap].reshape(slots, half2).astype(BF16)
+            sl = pl.ds(c * dc2 + side * half2, half2)
             first = jnp.dot(s0, piece, preferred_element_type=F32)
             second = jnp.dot(s1, piece, preferred_element_type=F32)
-            mixed = state[:, sl] + gates_ref[:, 0:1] * first + gates_ref[:, 1:2] * second
+            mixed = state[:, sl] + gate0 * first + gate1 * second
             out_ref[:, sl] = mixed.astype(BF16)
 
     order = [down_a, down_b, down_c, down_d]
-    for s in range(CHUNKS + len(order) - 1):
+    for s in range(BACK + len(order) - 1):
         for depth, stage in enumerate(order):
-            if 0 <= s - depth < CHUNKS:
+            if 0 <= s - depth < BACK:
                 stage(s - depth)
 
     for copy in sends:
@@ -361,7 +377,8 @@
     total = n_ten * slots
     ff = w_gate.shape[2]
     dc = width // CHUNKS
-    half = dc // 2
+    dc2 = width // BACK
+    half2 = dc2 // 2
     lanes = width // 2 + 128
     dma = pltpu.SemaphoreType.DMA
     hbm = pl.BlockSpec(memory_space=pl.ANY)
@@ -391,13 +408,13 @@
             pltpu.VMEM((total, ff), F32),
             pltpu.VMEM((total, ff), F32),
             pltpu.VMEM((total, ff), BF16),
-            pltpu.VMEM((CHUNKS, n_ten, slots, dc), F32),
-            pltpu.VMEM((CHUNKS, ny, slots, dc), BF16),
-            pltpu.VMEM((CHUNKS, ny, slots, dc), BF16),
-            pltpu.VMEM((CHUNKS, many, slots, dc), BF16),
-            pltpu.VMEM((CHUNKS, many, slots, dc), BF16),
-            pltpu.VMEM((CHUNKS, n_exp, 2 * cap, half), BF16),
-            pltpu.VMEM((CHUNKS, n_exp, 2 * cap, half), BF16),
+            pltpu.VMEM((BACK, n_ten, slots, dc2), F32),
+            pltpu.VMEM((BACK, ny, slots, dc2), BF16),
+            pltpu.VMEM((BACK, ny, slots, dc2), BF16),
+            pltpu.VMEM((BACK, many, slots, dc2), BF16),
+            pltpu.VMEM((BACK, many, slots, dc2), BF16),
+            pltpu.VMEM((BACK, n_exp, 2 * cap, half2), BF16),
+            pltpu.VMEM((BACK, n_exp, 2 * cap, half2), BF16),
             dma((2,)),
             dma((CHUNKS,)),
             dma((CHUNKS,)),
@@ -409,24 +426,24 @@
             dma((CHUNKS, many)),
             dma((CHUNKS, n_exp - 1)),
             dma((CHUNKS, n_exp - 1)),
-            dma((CHUNKS,)),
-            dma((CHUNKS,)),
-            dma((CHUNKS, many)),
-            dma((CHUNKS, many)),
-            dma((CHUNKS, many)),
-            dma((CHUNKS, many)),
-            dma((CHUNKS,)),
-            dma((CHUNKS,)),
-            dma((CHUNKS, many)),
-            dma((CHUNKS, many)),
-            dma((CHUNKS, n_exp - 1)),
-            dma((CHUNKS, n_exp - 1)),
+            dma((CHUNKS, n_exp)),
+            dma((CHUNKS, n_exp)),
+            dma((CHUNKS, n_exp, many)),
+            dma((CHUNKS, n_exp, many)),
+            dma((CHUNKS, n_exp, many)),
+            dma((CHUNKS, n_exp, many)),
+            dma((BACK,)),
+            dma((BACK,)),
+            dma((BACK, many)),
+            dma((BACK, many)),
+            dma((BACK, n_exp - 1)),
+            dma((BACK, n_exp - 1)),
         ],
         compiler_params=pltpu.CompilerParams(
             collective_id=0, has_side_effects=True, vmem_limit_bytes=62 * 1024 * 1024
         ),
     )(
-        context, out_proj, resid, norm_gain.reshape(1, width), routes, gates,
+        context, out_proj, resid, norm_gain, routes.T, gates.T,
         w_gate, w_up, w_down,
     )
 

time: 59.7 us -> 41.4 us (0.69)
  Pallas kernels: 53.8 us -> 39.7 us
  local copies, waits for them, and re-layouts: 5.57 us -> 1.54 us
    pallas_call x1, Pallas kernels: 53.8 us -> 39.7 us  [body(): pl.pallas_call(functools.partial(kernel, n_exp, n_ten), out_shape=jax.Sha...]
    unnamed x3 -> x1, local copies, waits for them, and re-layouts: 4.28 us -> 1.54 us
    reshape x1 -> x0, local copies, waits for them, and re-layouts: 1.3 us -> none  [body(): norm_gain.reshape(1, width)]
where the time goes in v2:
time: 41.4 us; the launch traced here: 41.2 us
  Pallas kernels  39.7 us (96%)
  local copies, waits for them, and re-layouts  1.54 us (4%)
    pallas_call x1, Pallas kernels, body(): pl.pallas_call(functools.partial(kernel, n_exp, n_ten), out_shape=jax.Sha...  39.7 us
    unnamed x1, local copies, waits for them, and re-layouts  1.54 us

profile of v2, /device:TPU:0, one launch (start us, length us, event | category | flops | bytes accessed | tf_op | source)
XLA Modules:
  0.0 41.2 jit_solution(6087100151214296629)
XLA Ops:
  0.0 39.7 %shard_map.91 = bf16[16,3072]{1,0:T(8,128)(2,1)} custom-call(bf16[64,768]{1,0:T(8,128)(2,1)} %ctx_hbm.1, bf16[768,3072]{1,0:T(8,128)(2,1)} %proj_hbm.1, bf16[64,3072]{1,0:T(8,128)(2,1)} %resid_hbm.1, bf16[3072]{0:T(1024)(128)(2,1)} %gain_ref.1, s32[2,64]{1,0:T(2,128)} %bitcast.2, f32[2,16]{1,0:T(2,128)} %bitcast.3, bf16[1,3072,2048]{2,1,0:T(8,128)(2,1)} %wg_hbm.1, ...), custom_call_target="tpu_custom_call" | custom-call | tf_op jit(solution)/shard_map/pallas_call | solution.py:387
  39.7 1.5 %copy.11 = bf16[16,3072]{1,0:T(8,128)(2,1)} copy(bf16[16,3072]{1,0:T(8,128)(2,1)} %shard_map.91) | data formatting | bytes 196608

commit v3 on v2

--- a/solution.py
+++ b/solution.py
@@ -166,7 +166,7 @@
         if c == 0:
             pl.semaphore_wait(barrier, 1 + (ny - 1) + (n_exp - 1))
         pa[c] = reduce_a(part, c, pa_out, pa_in, pas, par)
-        if c == CHUNKS - 1:
+        if c == 0:
             for load in [x for pair in zip(gate_loads, up_loads) for x in pair]:
                 load.start()
             down_load.start()
@@ -292,7 +292,7 @@
                     acc_u[at, cs_] = u
                 return 0
 
-            lax.fori_loop(0, ff // nt, tile, 0)
+            lax.fori_loop(0, ff // nt, tile, 0, unroll=True)
             return 0
 
         lax.fori_loop(0, total // mb, block, 0)

time: 41.4 us -> 40.1 us (0.969)
  Pallas kernels: 39.7 us -> 38.4 us
    pallas_call x1, Pallas kernels: 39.7 us -> 38.4 us  [body(): pl.pallas_call(functools.partial(kernel, n_exp, n_ten), out_shape=jax.Sha...]
where the time goes in v3:
time: 40.1 us; the launch traced here: 40 us
  Pallas kernels  38.4 us (96%)
  local copies, waits for them, and re-layouts  1.54 us (4%)
    pallas_call x1, Pallas kernels, body(): pl.pallas_call(functools.partial(kernel, n_exp, n_ten), out_shape=jax.Sha...  38.4 us
    unnamed x1, local copies, waits for them, and re-layouts  1.54 us

profile of v3, /device:TPU:0, one launch (start us, length us, event | category | flops | bytes accessed | tf_op | source)
XLA Modules:
  0.0 40.0 jit_solution(4216021460086900742)
XLA Ops:
  0.0 38.4 %shard_map.91 = bf16[16,3072]{1,0:T(8,128)(2,1)} custom-call(bf16[64,768]{1,0:T(8,128)(2,1)} %ctx_hbm.1, bf16[768,3072]{1,0:T(8,128)(2,1)} %proj_hbm.1, bf16[64,3072]{1,0:T(8,128)(2,1)} %resid_hbm.1, bf16[3072]{0:T(1024)(128)(2,1)} %gain_ref.1, s32[2,64]{1,0:T(2,128)} %bitcast.2, f32[2,16]{1,0:T(2,128)} %bitcast.3, bf16[1,3072,2048]{2,1,0:T(8,128)(2,1)} %wg_hbm.1, ...), custom_call_target="tpu_custom_call" | custom-call | tf_op jit(solution)/shard_map/pallas_call | solution.py:387
  38.4 1.5 %copy.11 = bf16[16,3072]{1,0:T(8,128)(2,1)} copy(bf16[16,3072]{1,0:T(8,128)(2,1)} %shard_map.91) | data formatting | bytes 196608
